TPU v7x, 32 devices: a whole 2x2x4 slice. The times are simulated.
32 devices in a mesh: req: 16 (over z, x, core), tp: 2 (over y).
Axes of the slice: x: 2, y: 2, z: 4, core: 2. Of those that a mesh axis runs over, the one named last changes fastest.
Arguments:
- tokens: bfloat16 [32, 512, 2048], P('req'), may hold values from -6 to 6
- qkv_master: float32 [2048, 3, 2048], P('req', None, 'tp')
- q_gain: float32 [2048], P('tp')
- k_gain: float32 [2048], P('tp')
- lengths: int32 [32], P('req'), may hold values from 1 to 512, as said below
- page_holder: int32 [32, 4], P('req'), may hold values from 0 to 15, as said below
- page_slot: int32 [32, 4], P('req'), may hold values from 0 to 2, as said below
Outputs:
- attended: bfloat16 [32, 512, 2048], P('req', None, 'tp')
- kv_cache: bfloat16 [144, 2, 128, 2048], P('req', None, None, 'tp')
Inputs may be any that keep to these rules, and one draw needn't show every extreme that they name: lengths[r] is at least 1; some prompt has exactly 512 tokens. page_holder[r, p] is r // 2, or the index just before or just after it along req, cyclically. The live pages of one req index's prompts that go to one holder have distinct page_slot values, so at most 3 of them; some req index sends 3 live pages to one holder.
All inputs are finite; a program needn't handle non-finite values.
Results may differ from a plain program's by a relative error of at most 0.009.
Values may be sent and summed in bfloat16 or wider, within the bound.
A program may use at most 128 MiB of HBM per device.

v0:
```python
import jax
import jax.numpy as jnp
from jax import lax
from jax.sharding import PartitionSpec as P

HD = 128
PAGE = 128
CAP = 3
SLOTS = 9


norm_epsilon = 1e-06
rope_theta = 500000.0


def extended(block, sides, width):
    for axis, dim in sides:
        count = lax.axis_size(axis)
        forward = [(i, i + 1) for i in range(count - 1)]
        forward.append((count - 1, 0))
        backward = [(target, source) for source, target in forward]
        low = lax.ppermute(
            lax.slice_in_dim(block, block.shape[dim] - width, None, axis=dim), axis, forward
        )
        high = lax.ppermute(lax.slice_in_dim(block, 0, width, axis=dim), axis, backward)
        block = jnp.concatenate([low, block, high], axis=dim)
    return block


def rotate(values_in, seq_len, head_size):
    half_size = head_size // 2
    positions = jnp.arange(seq_len).astype(jnp.float32)
    frequency = rope_theta ** (-jnp.arange(half_size).astype(jnp.float32) * 2.0 / head_size)
    angles = positions[:, None] * frequency[None, :]
    cosine_table = jnp.cos(angles)[:, None, :]
    sine_table = jnp.sin(angles)[:, None, :]
    front_half = values_in[..., :half_size]
    back_half = values_in[..., half_size:]
    return jnp.concatenate(
        [
            front_half * cosine_table - back_half * sine_table,
            back_half * cosine_table + front_half * sine_table,
        ],
        -1,
    )


def attend(request_item):
    queries, key_rows, value_rows, length = request_item
    seq_len = queries.shape[0]
    scores = jnp.einsum(
        "thd,uhd->htu", queries, key_rows, preferred_element_type=jnp.float32
    ) * HD ** (-0.5)
    query_pos = jnp.arange(seq_len)[:, None]
    key_pos = jnp.arange(seq_len)[None, :]
    allowed = (key_pos <= query_pos) & (key_pos < length)
    scores = jnp.where(allowed[None], scores, -1e30)
    row_max = jnp.max(scores, axis=-1, keepdims=True)
    exp_terms = jnp.where(allowed[None], jnp.exp(scores - row_max), 0.0)
    probs = (exp_terms / jnp.sum(exp_terms, axis=-1, keepdims=True)).astype(jnp.bfloat16)
    output = jnp.einsum("htu,uhd->thd", probs, value_rows, preferred_element_type=jnp.float32)
    keep_rows = jnp.arange(seq_len)[:, None, None] < length
    return jnp.where(keep_rows, output, 0.0).astype(jnp.bfloat16)


def body(tokens, qkv_master, q_gain, k_gain, lengths, page_holder, page_slot):
    req_dev, seq_len, model_width = tokens.shape
    row_share, _, q_local = qkv_master.shape
    heads_local = q_local // HD
    token_rows = tokens.reshape(req_dev * seq_len, model_width)
    master_local = qkv_master.astype(jnp.bfloat16).reshape(row_share, 3 * q_local)
    gathered = lax.all_gather(master_local, "req", axis=0, tiled=True)
    projected = jnp.dot(token_rows, gathered, preferred_element_type=jnp.float32)
    queries = projected[:, :q_local]
    key_rows = projected[:, q_local : 2 * q_local]
    values = projected[:, 2 * q_local :]
    square_sums = lax.psum((jnp.sum(queries * queries, -1), jnp.sum(key_rows * key_rows, -1)), "tp")
    full_width = q_local * lax.axis_size("tp")
    queries = queries * lax.rsqrt(square_sums[0] / full_width + norm_epsilon)[:, None] * q_gain
    key_rows = key_rows * lax.rsqrt(square_sums[1] / full_width + norm_epsilon)[:, None] * k_gain
    q_rot = rotate(queries.reshape(req_dev, seq_len, heads_local, HD), seq_len, HD).astype(
        jnp.bfloat16
    )
    k_rot = rotate(key_rows.reshape(req_dev, seq_len, heads_local, HD), seq_len, HD).astype(
        jnp.bfloat16
    )
    v_round = values.astype(jnp.bfloat16).reshape(req_dev, seq_len, heads_local, HD)
    attended = lax.map(attend, (q_rot, k_rot, v_round, lengths)).reshape(req_dev, seq_len, q_local)
    page_count = seq_len // PAGE
    home_index = lax.axis_index("req")
    axis_count = lax.axis_size("req")
    is_live = (jnp.arange(page_count) * PAGE)[None, :] < lengths[:, None]
    offset = (page_holder - home_index + 1 + axis_count) % axis_count - 1
    target = jnp.where(is_live, (offset + 1) * CAP + page_slot, -1).reshape(-1)
    onehot = (target[None, :] == jnp.arange(SLOTS)[:, None]).astype(jnp.bfloat16)
    stacked = jnp.stack(
        [
            k_rot.reshape(req_dev * page_count, PAGE * q_local),
            v_round.reshape(req_dev * page_count, PAGE * q_local),
        ],
        1,
    )
    stacked = stacked.reshape(req_dev * page_count, 2 * PAGE * q_local)
    outgoing = (
        jnp.dot(onehot, stacked, preferred_element_type=jnp.float32)
        .astype(jnp.bfloat16)
        .reshape(SLOTS, 2, PAGE, q_local)
    )
    padded = extended(outgoing, (("req", 0),), CAP)
    kv_cache = jnp.concatenate([padded[CAP + SLOTS :], outgoing[CAP : 2 * CAP], padded[:CAP]], 0)
    return (attended, kv_cache)


def solution(mesh):
    in_specs = (
        P("req", None, None),
        P("req", None, "tp"),
        P("tp"),
        P("tp"),
        P("req"),
        P("req", None),
        P("req", None),
    )
    out_specs = (P("req", None, "tp"), P("req", None, None, "tp"))
    return jax.shard_map(body, mesh=mesh, in_specs=in_specs, out_specs=out_specs, check_vma=False)
```

profile of v0, /device:TPU:1, one launch (start us, length us, event | category | flops | bytes accessed | tf_op | source)
XLA Modules:
  0.0 245.3 jit_solution(7315493069631317164)
XLA Ops:
  7.2 2.6 %copy.17 = bf16[128,3,1024]{0,2,1:T(8,128)(2,1)} copy(f32[128,3,1024]{2,0,1:T(8,128)} %param.10) | data formatting | bytes 2359296 | tf_op args[1]
  9.8 0.8 compare_select_fusion.2
  10.7 1.0 multiply_cosine_fusion
  11.7 105.5 %all-gather.2.cloned.1.call-done = bf16[2048,3072]{0,1:T(8,128)(2,1)} async-done(((bf16[128,3072]{0,1:T(8,128)(2,1)}), bf16[2048,3072]{0,1:T(8,128)(2,1)}) %all-gather.2.cloned.1.call-update) | async-done | bytes 12582928 | tf_op jit(solution)/shard_map/all_gather | solution.py:72
  117.2 17.1 %fusion.26 = f32[1024,3072]{1,0:T(8,128)S(1)} fusion(bf16[1024,2048]{1,0:T(8,128)(2,1)} %bitcast.66, bf16[2048,3072]{0,1:T(8,128)(2,1)} %all-gather.2.cloned.1.call-done), kind=kOutput, calls=%fused_computation.60 | convolution fusion | flops 12884901888 | bytes 29360128 | tf_op jit(solution)/shard_map/dot_general | solution.py:73
  134.3 0.6 multiply_reduce_fusion
  134.9 0.5 slice_bitcast_fusion
  135.5 3.4 %copy-done.1 = f32[1024,3072]{1,0:T(8,128)} copy-done((f32[1024,3072]{1,0:T(8,128)}, f32[1024,3072]{1,0:T(8,128)S(1)}, u32[]{:S(2)}) %copy-start.1) | copy-done | bytes 12582936
  139.2 1.9 copy.32
  141.2 3.8 %all-reduce = (f32[1024]{0:T(1024)S(1)}, f32[1024]{0:T(1024)S(1)}) all-reduce(f32[1024]{0:T(1024)S(1)} %get-tuple-element.48, f32[1024]{0:T(1024)S(1)} %get-tuple-element.47), channel_id=1, replica_groups=mesh['req'=16,'tp'=2] {'tp'}, use_global_device_ids=true, to_apply=%region_1.0 | all-reduce | flops 2048 | bytes 16384 | tf_op jit(solution)/shard_map/psum | solution.py:77
  145.0 5.3 %multiply_bitcast_fusion = (f32[128,8,8,128]{3,1,2,0:T(8,128)S(1)}, f32[128,8,8,128]{3,1,2,0:T(8,128)}) fusion(f32[1024,3072]{1,0:T(8,128)} %copy-done.1, f32[1024]{0:T(1024)S(1)} %copy-done.8, f32[1024]{0:T(1024)S(1)} %get-tuple-element.80, f32[1024]{0:T(1024)S(1)} %copy-done.9, f32[1024]{0:T(1024)S(1)} %get-tuple-element.81), kind=kLoop, calls=%fused_computation.32 | loop fusion | flops 4194304 | bytes 16793600
  150.3 3.0 %copy.34 = f32[128,8,8,128]{3,2,1,0:T(8,128)} copy(f32[128,8,8,128]{3,1,2,0:T(8,128)S(1)} %get-tuple-element.65) | data formatting | bytes 8388608
  153.2 2.3 stack_reshape_reshape.3
  155.5 3.2 %copy.33 = f32[128,8,8,128]{3,2,1,0:T(8,128)S(1)} copy(f32[128,8,8,128]{3,1,2,0:T(8,128)} %get-tuple-element.66) | data formatting | bytes 8388608
  158.7 4.7 %fusion.25 = (f32[2,512,8,64]{3,2,1,0:T(8,128)}, f32[2,512,8,64]{3,2,1,0:T(8,128)}) fusion(f32[2,512,8,128]{3,2,1,0:T(8,128)S(1)} %bitcast.57), kind=kLoop, calls=%fused_computation.58 | loop fusion | bytes 8388608 | tf_op jit(solution)/shard_map/slice | solution.py:37
  163.4 1.3 fusion.24
  164.8 1.7 multiply_subtract_fusion
  166.4 1.2 maximum_convert_fusion
  167.6 2.7 %copy.24 = bf16[2,512,8,128]{3,2,1,0:T(8,128)(2,1)} copy(bf16[2,512,8,128]{3,1,2,0:T(8,128)(2,1)S(1)} %maximum_convert_fusion) | data formatting | bytes 4194304 | tf_op jit(solution)/shard_map/convert_element_type | solution.py:84
  170.3 3.8 %convert_element_type.79 = bf16[8,1,131072]{2,0,1:T(8,128)(2,1)} reshape(bf16[2,512,8,128]{3,2,1,0:T(8,128)(2,1)} %copy.24) | data formatting | bytes 4194304 | tf_op jit(solution)/shard_map/convert_element_type | solution.py:84
  174.1 2.6 %pad_maximum_fusion.1 = bf16[8,2,131072]{2,0,1:T(8,128)(2,1)S(1)} fusion(bf16[8,1,131072]{2,0,1:T(8,128)(2,1)} %stack_reshape_reshape.3, bf16[8,1,131072]{2,0,1:T(8,128)(2,1)} %convert_element_type.79), kind=kLoop, calls=%fused_computation.29 | loop fusion | flops 2097152 | bytes 8388608 | tf_op jit(solution)/shard_map/stack | solution.py:96
  176.7 2.6 %convolution_convert_fusion = bf16[9,262144]{1,0:T(8,128)(2,1)S(1)} fusion(bf16[8,262144]{1,0:T(8,128)(2,1)S(1)} %bitcast.59, s32[8]{0:T(128)S(1)} %eq.17), kind=kOutput, calls=%fused_computation.25 | convolution fusion | flops 40108104 | bytes 8912928 | tf_op jit(solution)/shard_map/dot_general | solution.py:105
  179.3 3.5 %fusion.23 = (bf16[3,262144]{1,0:T(4,128)(2,1)S(1)}, bf16[3,262144]{1,0:T(4,128)(2,1)S(1)}, bf16[3,262144]{1,0:T(4,128)(2,1)}) fusion(bf16[9,262144]{1,0:T(8,128)(2,1)S(1)} %convolution_convert_fusion), kind=kLoop, calls=%fused_computation.56 | loop fusion | bytes 9437184 | tf_op jit(solution)/shard_map/slice | solution.py:25
  182.8 1.8 copy.35
  184.5 1.8 copy.37
  186.3 2.5 %collective-permute-start.1 = (bf16[3,2,128,1024]{3,2,1,0:T(8,128)(2,1)}, bf16[3,2,128,1024]{3,2,1,0:T(8,128)(2,1)}, u32[]{:S(2)}, u32[]{:S(2)}) collective-permute-start(bf16[3,2,128,1024]{3,2,1,0:T(8,128)(2,1)} %bitcast.29), channel_id=1, source_target_pairs={{0,2},{2,4},{4,6},{6,8},{8,10},{10,12},{12,14},{14,16},{16,18},{18... | collective-permute-start | bytes 4718600 | tf_op jit(solution)/shard_map/ppermute | solution.py:22
  188.8 1.7 subtract_convert_fusion
  190.5 2.5 %pad_maximum_fusion.2 = bf16[2,512,8,128]{3,1,2,0:T(8,128)(2,1)} fusion(bf16[2,512,8,64]{3,1,2,0:T(8,128)(2,1)S(1)} %get-tuple-element.70, bf16[2,512,8,64]{3,1,2,0:T(8,128)(2,1)S(1)} %get-tuple-element.69), kind=kLoop, calls=%fused_computation.38 | loop fusion | flops 4194304 | bytes 4194304 | tf_op jit(solution)/shard_map/concatenate | solution.py:39
  192.9 37.0 %while.10 = (s32[]{:T(128)}, bf16[2,512,8,128]{1,3,2,0:T(8,128)(2,1)}, s32[2]{0:T(128)S(1)}, bf16[2,512,8,128]{3,2,1,0:T(8,128)(2,1)}, bf16[2,512,8,128]{3,1,2,0...) while((s32[]{:T(128)}, bf16[2,512,8,128]{1,3,2,0:T(8,128)(2,1)}, s32[2]{0:T(128)S(1)}, ...), condition=%wide.region_7.8_spmd, body=%wide.region_4.7_spmd.sunk | while | flops 1094190080 | bytes 63474368 | solution.py:88
  192.9 0.6 dynamic_slice.30
  193.5 0.6 iota_compare_fusion.5
  194.3 1.3 constant_dynamic-slice_fusion.2
  195.6 1.5 copy.47
  197.1 2.5 %fusion.40 = f32[8,512,512]{1,2,0:T(8,128)S(1)} fusion(bf16[2,512,8,128]{3,1,2,0:T(8,128)(2,1)S(1)} %get-tuple-element.142, s32[]{:T(128)S(6)} %copy.51, bf16[2,512,8,128]{3,1,2,0:T(8,128)(2,1)} %get-tuple-element.141), kind=kOutput, calls=%fused_computation.12.clone.1 | convolution fusion | flops 536870912 | bytes 10486784 | tf_op jit(solution)/shard_map/while/body/eval_jaxpr/thd,uhd->htu/dot_general | solution.py:51
  199.6 6.3 %fusion.42 = (f32[8,512]{1,0:T(8,128)S(1)}, f32[8,512,512]{1,2,0:T(8,128)}) fusion(f32[8,512,512]{1,2,0:T(8,128)S(1)} %fusion.40, pred[512,512]{0,1:T(8,128)(4,1)S(1)} %fusion.41), kind=kOutput, calls=%fused_computation.55.clone.1 | output fusion | flops 14680575 | bytes 17055744 | tf_op jit(solution)/shard_map/while/body/eval_jaxpr/sub | solution.py:59
  205.9 4.2 %fusion.43 = bf16[2,512,8,128]{1,3,2,0:T(8,128)(2,1)S(1)} fusion(bf16[2,512,8,128]{1,3,2,0:T(8,128)(2,1)S(1)} %copy-done.6, s32[]{:T(128)S(6)} %copy.51, f32[8,512,512]{1,2,0:T(8,128)} %get-tuple-element.121, f32[8,512]{1,0:T(8,128)S(1)} %get-tuple-element.122, bf16[1,512,8,128]{1,3,2,0:T(8,128)(2,1)S(1)} %copy-done.2, ...), kind=kOutput, calls=%fused_computation.11.clone.1 | convolution fusion | flops 542113792 | bytes 10502660 | tf_op jit(solution)/shard_map/while/body/eval_jaxpr/htu,uhd->thd/dot_general | solution.py:61
  210.1 1.3 copy-done.7
  211.4 0.6 dynamic_slice.30
  212.0 0.6 iota_compare_fusion.5
  212.8 1.3 constant_dynamic-slice_fusion.2
  214.1 1.5 copy.47
  215.6 2.5 %fusion.40 = f32[8,512,512]{1,2,0:T(8,128)S(1)} fusion(bf16[2,512,8,128]{3,1,2,0:T(8,128)(2,1)S(1)} %get-tuple-element.142, s32[]{:T(128)S(6)} %copy.51, bf16[2,512,8,128]{3,1,2,0:T(8,128)(2,1)} %get-tuple-element.141), kind=kOutput, calls=%fused_computation.12.clone.1 | convolution fusion | flops 536870912 | bytes 10486784 | tf_op jit(solution)/shard_map/while/body/eval_jaxpr/thd,uhd->htu/dot_general | solution.py:51
  218.1 6.3 %fusion.42 = (f32[8,512]{1,0:T(8,128)S(1)}, f32[8,512,512]{1,2,0:T(8,128)}) fusion(f32[8,512,512]{1,2,0:T(8,128)S(1)} %fusion.40, pred[512,512]{0,1:T(8,128)(4,1)S(1)} %fusion.41), kind=kOutput, calls=%fused_computation.55.clone.1 | output fusion | flops 14680575 | bytes 17055744 | tf_op jit(solution)/shard_map/while/body/eval_jaxpr/sub | solution.py:59
  224.4 4.2 %fusion.43 = bf16[2,512,8,128]{1,3,2,0:T(8,128)(2,1)S(1)} fusion(bf16[2,512,8,128]{1,3,2,0:T(8,128)(2,1)S(1)} %copy-done.6, s32[]{:T(128)S(6)} %copy.51, f32[8,512,512]{1,2,0:T(8,128)} %get-tuple-element.121, f32[8,512]{1,0:T(8,128)S(1)} %get-tuple-element.122, bf16[1,512,8,128]{1,3,2,0:T(8,128)(2,1)S(1)} %copy-done.2, ...), kind=kOutput, calls=%fused_computation.11.clone.1 | convolution fusion | flops 542113792 | bytes 10502660 | tf_op jit(solution)/shard_map/while/body/eval_jaxpr/htu,uhd->thd/dot_general | solution.py:61
  228.6 1.3 copy-done.7
  229.9 4.1 %copy.26 = bf16[2,512,1024]{2,1,0:T(8,128)(2,1)} copy(bf16[2,512,1024]{1,2,0:T(8,128)(2,1)} %bitcast.65) | data formatting | bytes 4194304 | tf_op jit(solution)/shard_map/reshape | solution.py:88
  234.0 0.6 copy.36
  234.6 3.8 %pad_maximum_fusion = bf16[9,2,128,1024]{3,2,1,0:T(8,128)(2,1)} fusion(bf16[3,2,128,1024]{3,2,1,0:T(8,128)(2,1)} %collective-permute-done.1, bf16[3,2,128,1024]{3,2,1,0:T(8,128)(2,1)S(1)} %bitcast.63, bf16[3,2,128,1024]{3,2,1,0:T(8,128)(2,1)} %collective-permute-done), kind=kLoop, calls=%fused_computation.26 | loop fusion | flops 4718592 | bytes 9437184 | tf_op jit(solution)/shard_map/concatenate | solution.py:110
  (39 shorter events, 0.8 us)
Async XLA Ops:
  7.2 110.0 %all-gather.2.cloned.1.call-start = ((), (), s32[]{:S(2)}) async-start(), calls=%async_computation | async-start | bytes 13369344 | tf_op jit(solution)/shard_map/all_gather | solution.py:72
  134.3 4.6 %copy-start.1 = (f32[1024,3072]{1,0:T(8,128)}, f32[1024,3072]{1,0:T(8,128)S(1)}, u32[]{:S(2)}) copy-start(f32[1024,3072]{1,0:T(8,128)S(1)} %fusion.26) | copy-start | bytes 37748740
  138.9 6.1 %copy-start.8 = (f32[1024]{0:T(1024)S(1)}, f32[1024]{0:T(1024)}, u32[]{:S(2)}) copy-start(f32[1024]{0:T(1024)} %param.12) | copy-start | bytes 12292
  138.9 6.1 %copy-start.9 = (f32[1024]{0:T(1024)S(1)}, f32[1024]{0:T(1024)}, u32[]{:S(2)}) copy-start(f32[1024]{0:T(1024)} %param.11) | copy-start | bytes 12292
  158.7 4.7 %copy-start = (f32[128,8,8,128]{3,2,1,0:T(8,128)S(1)}, f32[128,8,8,128]{3,2,1,0:T(8,128)}, u32[]{:S(2)}) copy-start(f32[128,8,8,128]{3,2,1,0:T(8,128)} %copy.34) | copy-start | bytes 12582916
  179.3 9.5 %copy-start.4 = (f32[2,512,8,64]{3,2,1,0:T(8,128)S(1)}, f32[2,512,8,64]{3,2,1,0:T(8,128)}, u32[]{:S(2)}) copy-start(f32[2,512,8,64]{3,2,1,0:T(8,128)} %get-tuple-element.77) | copy-start | bytes 6291460
  182.8 6.0 %copy-start.3 = (f32[2,512,8,64]{3,2,1,0:T(8,128)S(1)}, f32[2,512,8,64]{3,2,1,0:T(8,128)}, u32[]{:S(2)}) copy-start(f32[2,512,8,64]{3,2,1,0:T(8,128)} %get-tuple-element.76) | copy-start | bytes 6291460
  186.3 48.3 %collective-permute-start.1 = (bf16[3,2,128,1024]{3,2,1,0:T(8,128)(2,1)}, bf16[3,2,128,1024]{3,2,1,0:T(8,128)(2,1)}, u32[]{:S(2)}, u32[]{:S(2)}) collective-permute-start(bf16[3,2,128,1024]{3,2,1,0:T(8,128)(2,1)} %bitcast.29), channel_id=1, source_target_pairs={{0,2},{2,4},{4,6},{6,8},{8,10},{10,12},{12,14},{14,16},{16,18},{18... | collective-permute-start | bytes 4718600 | tf_op jit(solution)/shard_map/ppermute | solution.py:22
  188.8 45.8 %collective-permute-start = (bf16[3,2,128,1024]{3,2,1,0:T(8,128)(2,1)}, bf16[3,2,128,1024]{3,2,1,0:T(8,128)(2,1)}, u32[]{:S(2)}, u32[]{:S(2)}) collective-permute-start(bf16[3,2,128,1024]{3,2,1,0:T(8,128)(2,1)} %bitcast.23), channel_id=1, source_target_pairs={{2,0},{4,2},{6,4},{8,6},{10,8},{12,10},{14,12},{16,14},{18,16},{20... | collective-permute-start | bytes 4718600 | tf_op jit(solution)/shard_map/ppermute | solution.py:25
  190.4 2.5 %copy-start.10 = (s32[2]{0:T(128)S(1)}, s32[2]{0:T(128)}, u32[]{:S(2)}) copy-start(s32[2]{0:T(128)} %param.13) | copy-start | bytes 28
  199.6 6.3 %copy-start.2 = (bf16[1,512,8,128]{1,3,2,0:T(8,128)(2,1)S(1)}, bf16[1,512,8,128]{1,3,2,0:T(8,128)(2,1)}, u32[]{:S(2)}) copy-start(bf16[1,512,8,128]{1,3,2,0:T(8,128)(2,1)} %copy.47) | copy-start | bytes 3145732 | tf_op jit(solution)/shard_map/while
  199.6 6.3 %copy-start.6 = (bf16[2,512,8,128]{1,3,2,0:T(8,128)(2,1)S(1)}, bf16[2,512,8,128]{1,3,2,0:T(8,128)(2,1)}, u32[]{:S(2)}) copy-start(bf16[2,512,8,128]{1,3,2,0:T(8,128)(2,1)} %get-tuple-element.131) | copy-start | bytes 6291460 | tf_op jit(solution)/shard_map/while
  210.1 1.3 copy-start.7
  218.1 6.3 %copy-start.2 = (bf16[1,512,8,128]{1,3,2,0:T(8,128)(2,1)S(1)}, bf16[1,512,8,128]{1,3,2,0:T(8,128)(2,1)}, u32[]{:S(2)}) copy-start(bf16[1,512,8,128]{1,3,2,0:T(8,128)(2,1)} %copy.47) | copy-start | bytes 3145732 | tf_op jit(solution)/shard_map/while
  218.1 6.3 %copy-start.6 = (bf16[2,512,8,128]{1,3,2,0:T(8,128)(2,1)S(1)}, bf16[2,512,8,128]{1,3,2,0:T(8,128)(2,1)}, u32[]{:S(2)}) copy-start(bf16[2,512,8,128]{1,3,2,0:T(8,128)(2,1)} %get-tuple-element.131) | copy-start | bytes 6291460 | tf_op jit(solution)/shard_map/while
  228.6 1.3 copy-start.7
  229.9 4.1 %copy-start.5 = (bf16[3,262144]{1,0:T(4,128)(2,1)S(1)}, bf16[3,262144]{1,0:T(4,128)(2,1)}, u32[]{:S(2)}) copy-start(bf16[3,262144]{1,0:T(4,128)(2,1)} %get-tuple-element.73) | copy-start | bytes 4718596
Sparse Core Ops, SparseCore 0:
  10.7 106.4 all-gather.1
where the time goes:
time: 249 us; the launch traced here: 245 us
  waiting for transfers between devices  106 us (43%)
  local copies, waits for them, and re-layouts  51 us (20%)
  other arithmetic  35.2 us (14%)
  matrix products  33 us (13%)
  between operations  14.2 us (6%)
  blocking collectives  3.82 us (2%)
  starting transfers between devices  2.5 us (1%)
    all_gather x1, waiting for transfers between devices, body(): gathered = lax.all_gather(master_local, 'req', axis=0, tiled=True)  106 us
    unnamed x24, local copies, waits for them, and re-layouts  18.8 us
    dot_general x1, matrix products, body(): jnp.dot(token_rows, gathered, preferred_element_type=jnp.float32)  17.1 us
    sub x2, other arithmetic, attend(): exp_terms = jnp.where(allowed[None], jnp.exp(scores - row_max), 0.0)  12.6 us
    dot_general x2, matrix products, attend(): jnp.einsum('htu,uhd->thd', probs, value_rows, preferred_element_type=jnp....  8.38 us
    dynamic_slice x6, local copies, waits for them, and re-layouts, body(): lax.map(attend, (q_rot, k_rot, v_round, lengths))  6.79 us
    convert_element_type x2, local copies, waits for them, and re-layouts, body(): rotate(key_rows.reshape(req_dev, seq_len, heads_local, HD), seq_len, HD)  6.5 us
    slice x2, local copies, waits for them, and re-layouts, rotate(): front_half = values_in[..., :half_size]  6.05 us
  transfers between devices with their start and end apart: 3, of which 1 were waited for; matrix products, arithmetic and copies ran while one was open for 18% of the time, Pallas kernels for 0%

commit v1 on v0

v1 whole, which is shorter than its diff:
```python
import functools

import jax
import jax.numpy as jnp
from jax import lax
from jax.experimental import pallas as pl
from jax.experimental.pallas import tpu as pltpu
from jax.sharding import PartitionSpec as P

HD = 128
PAGE = 128
CAP = 3
SLOTS = 9
STREAMS = 6
MESH = pl.DeviceIdType.MESH
VMEM_LIMIT = 56 * 1024 * 1024

norm_epsilon = 1e-06
rope_theta = 500000.0


def project_kernel(
    n, full_width, seq_len,
    tok, wown, cos_t, sin_t, q_gain, k_gain,
    q_out, k_out, v_out,
    weight, acc, ss_local, ss_remote,
    ring_send, ring_recv, sib_send, sib_recv, x_send, x_recv,
):
    rows = wown.shape[1]
    half = wown.shape[2]
    token_rows, width = tok.shape
    chips = n // 2
    column = chips // 2
    me, tp = lax.axis_index("req"), lax.axis_index("tp")
    chip, core = me // 2, me % 2
    side, level = chip % 2, chip // 2
    place = level * (1 - side) + (chips - 1 - level) * side

    def chip_at(position):
        p = (position + 2 * chips) % chips
        u = p // column
        return 2 * (p * (1 - u) + (chips - 1 - p) * u) + u

    following = (chip_at(place + 1) * 2 + core, tp)
    preceding = (chip_at(place - 1) * 2 + core, tp)
    sibling = (chip * 2 + 1 - core, tp)
    other = (me, 1 - tp)
    onward = (following, preceding)

    def owner(direction, step):
        return chip_at(place - step + 2 * direction * step)

    def chunk(u, chip_index, core_index):
        start = pl.multiple_of((chip_index * 2 + core_index) * rows, 16)
        return weight.at[u, pl.ds(start, rows), :]

    def ring(u, step):
        piece = chunk(u, owner(u % 2, step - 1), core)
        return pltpu.make_async_remote_copy(
            piece, piece, ring_send.at[u, step], ring_recv.at[u, step],
            device_id=onward[u % 2], device_id_type=MESH,
        )

    def ring_in(u, step):
        piece = chunk(u, owner(u % 2, step), core)
        return pltpu.make_async_remote_copy(
            piece, piece, ring_send.at[u, step], ring_recv.at[u, step],
            device_id=onward[u % 2], device_id_type=MESH,
        )

    def sib(u, step, whose):
        piece = chunk(u, owner(u % 2, step), whose)
        return pltpu.make_async_remote_copy(
            piece, piece, sib_send.at[u, step], sib_recv.at[u, step],
            device_id=sibling, device_id_type=MESH,
        )

    fused = (2 * rows) % 256 == 0
    tile = 256

    def multiply(step, first):
        for u in range(STREAMS):
            sib(u, step, 1 - core).wait_recv()
            if not fused:
                continue
            start = pl.multiple_of(owner(u % 2, step) * 2 * rows, 256)

            def one(i, carry, u=u, start=start):
                at = pl.multiple_of(i * tile, tile)
                part = jnp.dot(
                    tok[pl.ds(at, tile), pl.ds(start, 2 * rows)],
                    weight[u, pl.ds(start, 2 * rows), :],
                    preferred_element_type=jnp.float32,
                )
                if first:
                    acc[u, pl.ds(at, tile), :] = part
                else:
                    acc[u, pl.ds(at, tile), :] += part
                return carry

            lax.fori_loop(0, token_rows // tile, one, 0)

    own_start = pl.multiple_of(me * rows, 16)
    for u in range(STREAMS):
        weight[u, pl.ds(own_start, rows), :] = wown[u]

    barrier = pltpu.get_barrier_semaphore()
    for device in (following, preceding, sibling, other):
        pl.semaphore_signal(barrier, inc=1, device_id=device, device_id_type=MESH)
    pl.semaphore_wait(barrier, 4)

    for u in range(STREAMS):
        ring(u, 1).start()
    for u in range(STREAMS):
        sib(u, 0, core).start()
    multiply(0, True)

    def middle(step, carry):
        for u in range(STREAMS):
            ring_in(u, step).wait_recv()
            ring(u, step + 1).start()
            sib(u, step, core).start()
        multiply(step, False)
        return carry

    lax.fori_loop(1, chips - 1, middle, 0)
    last = chips - 1
    for u in range(STREAMS):
        ring_in(u, last).wait_recv()
        sib(u, last, core).start()
    multiply(last, False)

    if not fused:
        for u in range(STREAMS):

            def whole(i, carry, u=u):
                at = pl.multiple_of(i * tile, tile)
                acc[u, pl.ds(at, tile), :] = jnp.dot(
                    tok[pl.ds(at, tile), :], weight[u], preferred_element_type=jnp.float32
                )
                return carry

            lax.fori_loop(0, token_rows // tile, whole, 0)

    block = 128
    lanes = lax.broadcasted_iota(jnp.int32, (block, 128), 1)

    def squares(i, carry):
        at = pl.multiple_of(i * block, block)

        def total(first_stream):
            a = acc[first_stream, pl.ds(at, block), :]
            b = acc[first_stream + 1, pl.ds(at, block), :]
            return jnp.sum(a * a + b * b, axis=-1, keepdims=True)

        placed = jnp.where(lanes == 0, total(4), jnp.where(lanes == 1, total(0), 0.0))
        ss_local[:, pl.ds(at, block)] = placed.T[:8, :]
        return carry

    lax.fori_loop(0, token_rows // block, squares, 0)
    exchange = pltpu.make_async_remote_copy(
        ss_local, ss_remote, x_send, x_recv, device_id=other, device_id_type=MESH
    )
    exchange.start()

    def write_values(i, carry):
        at = pl.multiple_of(i * block, block)
        for part in range(2):
            v_out[pl.ds(at, block), part * half : (part + 1) * half] = acc[
                2 + part, pl.ds(at, block), :
            ].astype(jnp.bfloat16)
        return carry

    lax.fori_loop(0, token_rows // block, write_values, 0)
    exchange.wait()

    def turn(i, carry):
        at = pl.multiple_of(i * block, block)
        spot = pl.multiple_of((i * block) % seq_len, block)
        sums = ss_local[:, pl.ds(at, block)] + ss_remote[:, pl.ds(at, block)]
        scale = lax.rsqrt(sums / full_width + norm_epsilon)
        scale = jnp.concatenate([scale, jnp.zeros((block - 8, 128), jnp.float32)], 0).T
        cosine = cos_t[pl.ds(spot, block), :]
        sine = sin_t[pl.ds(spot, block), :]
        for base, lane, gain, out in ((4, 0, q_gain, q_out), (0, 1, k_gain, k_out)):
            factor = scale[:, lane : lane + 1]
            for part in range(2):
                for c in range(half // HD):
                    h = slice(part * half + c * HD, part * half + (c + 1) * HD)
                    x = acc[base + part, pl.ds(at, block), c * HD : (c + 1) * HD]
                    x = x * factor * gain[:, h]
                    y = x * cosine + pltpu.roll(x, HD // 2, 1) * sine
                    out[pl.ds(at, block), h] = y.astype(jnp.bfloat16)
        return carry

    lax.fori_loop(0, token_rows // block, turn, 0)

    def drain(step, carry):
        for u in range(STREAMS):
            ring(u, step).wait_send()
        return carry

    lax.fori_loop(1, chips, drain, 0)

    def drain_sib(step, carry):
        for u in range(STREAMS):
            sib(u, step, core).wait_send()
        return carry

    lax.fori_loop(0, chips, drain_sib, 0)


def attention_kernel(lengths, q, k, v, out):
    length = lengths[pl.program_id(0)]
    seq_len = q.shape[0]
    step = 128
    for h in range(q.shape[1] // HD):
        hs = slice(h * HD, (h + 1) * HD)
        for b in range(seq_len // step):
            rows, count = slice(b * step, (b + 1) * step), (b + 1) * step
            scores = lax.dot_general(
                q[rows, hs], k[:count, hs], (((1,), (1,)), ((), ())),
                preferred_element_type=jnp.float32,
            ) * HD ** (-0.5)
            query_pos = lax.broadcasted_iota(jnp.int32, (step, count), 0) + b * step
            key_pos = lax.broadcasted_iota(jnp.int32, (step, count), 1)
            allowed = (key_pos <= query_pos) & (key_pos < length)
            scores = jnp.where(allowed, scores, -1e30)
            top = jnp.max(scores, axis=-1, keepdims=True)
            terms = jnp.exp(scores - top)
            total = jnp.sum(terms, axis=-1, keepdims=True)
            mixed = jnp.dot(
                terms.astype(jnp.bfloat16), v[:count, hs], preferred_element_type=jnp.float32
            ) / total
            row = lax.broadcasted_iota(jnp.int32, (step, HD), 0) + b * step
            out[rows, hs] = jnp.where(row < length, mixed, 0.0).astype(jnp.bfloat16)


def pack_kernel(index, valid, k, v, out):
    keep = valid[pl.program_id(0)] > 0
    zero = jnp.zeros(k.shape, k.dtype)
    out[0, 0] = jnp.where(keep, k[...], zero)
    out[0, 1] = jnp.where(keep, v[...], zero)


def pack(k, v, index, valid):
    width = k.shape[1]
    return pl.pallas_call(
        pack_kernel,
        grid_spec=pltpu.PrefetchScalarGridSpec(
            num_scalar_prefetch=2,
            grid=(CAP,),
            in_specs=[pl.BlockSpec((PAGE, width), lambda s, index, valid: (index[s], 0))] * 2,
            out_specs=pl.BlockSpec((1, 2, PAGE, width), lambda s, index, valid: (s, 0, 0, 0)),
        ),
        out_shape=jax.ShapeDtypeStruct((CAP, 2, PAGE, width), k.dtype),
    )(index, valid, k, v)


def assemble_kernel(index, valid, k, v, low, high, out):
    s = pl.program_id(0)
    keep = valid[s] > 0

    @pl.when(s < CAP)
    def _():
        out[...] = high[...]

    @pl.when((s >= CAP) & (s < 2 * CAP))
    def _():
        zero = jnp.zeros(k.shape, k.dtype)
        out[0, 0] = jnp.where(keep, k[...], zero)
        out[0, 1] = jnp.where(keep, v[...], zero)

    @pl.when(s >= 2 * CAP)
    def _():
        out[...] = low[...]


def assemble(k, v, low, high, index, valid):
    width = k.shape[1]
    own = jnp.concatenate([jnp.full((CAP,), index[CAP]), index[CAP : 2 * CAP], jnp.full((CAP,), index[2 * CAP - 1])])
    block = (1, 2, PAGE, width)
    page = pl.BlockSpec((PAGE, width), lambda s, index, valid: (index[s], 0))
    return pl.pallas_call(
        assemble_kernel,
        grid_spec=pltpu.PrefetchScalarGridSpec(
            num_scalar_prefetch=2,
            grid=(SLOTS,),
            in_specs=[
                page,
                page,
                pl.BlockSpec(block, lambda s, index, valid: (jnp.maximum(s - 2 * CAP, 0), 0, 0, 0)),
                pl.BlockSpec(block, lambda s, index, valid: (jnp.minimum(s, CAP - 1), 0, 0, 0)),
            ],
            out_specs=pl.BlockSpec(block, lambda s, index, valid: (s, 0, 0, 0)),
        ),
        out_shape=jax.ShapeDtypeStruct((SLOTS, 2, PAGE, width), k.dtype),
    )(own, valid, k, v, low, high)


def body(tokens, qkv_master, q_gain, k_gain, lengths, page_holder, page_slot):
    req_dev, seq_len, model_width = tokens.shape
    row_share, _, q_local = qkv_master.shape
    half = q_local // 2
    count = lax.axis_size("req")
    chips = count // 2
    token_rows = tokens.reshape(req_dev * seq_len, model_width)
    own = jnp.concatenate([qkv_master[:, 1:], qkv_master[:, :1]], 1).astype(jnp.bfloat16)
    own = own.reshape(row_share, STREAMS, half).transpose(1, 0, 2)

    frequency = rope_theta ** (-jnp.arange(HD // 2).astype(jnp.float32) * 2.0 / HD)
    angles = jnp.arange(seq_len).astype(jnp.float32)[:, None] * frequency[None, :]
    cosine, sine = jnp.cos(angles), jnp.sin(angles)
    cosine = jnp.concatenate([cosine, cosine], -1)
    sine = jnp.concatenate([-sine, sine], -1)

    vmem = pl.BlockSpec(memory_space=pltpu.VMEM)
    flat = jax.ShapeDtypeStruct((req_dev * seq_len, q_local), jnp.bfloat16)
    q, k, v = pl.pallas_call(
        functools.partial(project_kernel, count, q_local * lax.axis_size("tp"), seq_len),
        out_shape=(flat, flat, flat),
        in_specs=[vmem] * 6,
        out_specs=(vmem, vmem, vmem),
        scratch_shapes=[
            pltpu.VMEM((STREAMS, model_width, half), jnp.bfloat16),
            pltpu.VMEM((STREAMS, req_dev * seq_len, half), jnp.float32),
            pltpu.VMEM((8, req_dev * seq_len), jnp.float32),
            pltpu.VMEM((8, req_dev * seq_len), jnp.float32),
            pltpu.SemaphoreType.DMA((STREAMS, chips)),
            pltpu.SemaphoreType.DMA((STREAMS, chips)),
            pltpu.SemaphoreType.DMA((STREAMS, chips)),
            pltpu.SemaphoreType.DMA((STREAMS, chips)),
            pltpu.SemaphoreType.DMA,
            pltpu.SemaphoreType.DMA,
        ],
        compiler_params=pltpu.CompilerParams(
            collective_id=0, has_side_effects=True, vmem_limit_bytes=VMEM_LIMIT
        ),
    )(token_rows, own, cosine, sine, q_gain[None, :], k_gain[None, :])

    page_count = seq_len // PAGE
    home = lax.axis_index("req")
    live = (jnp.arange(page_count) * PAGE)[None, :] < lengths[:, None]
    offset = (page_holder - home + 1 + count) % count - 1
    target = jnp.where(live, (offset + 1) * CAP + page_slot, -1).reshape(-1)
    match = target[None, :] == jnp.arange(SLOTS)[:, None]
    valid = jnp.any(match, 1).astype(jnp.int32)
    index = jnp.sum(match * jnp.arange(req_dev * page_count)[None, :], 1).astype(jnp.int32)

    forward = [(i, (i + 1) % count) for i in range(count)]
    backward = [(j, i) for i, j in forward]
    low = lax.ppermute(pack(k, v, index[2 * CAP :], valid[2 * CAP :]), "req", forward)
    high = lax.ppermute(pack(k, v, index[:CAP], valid[:CAP]), "req", backward)

    heads = q_local // HD
    group = 4
    spec = pl.BlockSpec((seq_len, group * HD), lambda r, h, lengths: (r, h))
    attended = pl.pallas_call(
        attention_kernel,
        grid_spec=pltpu.PrefetchScalarGridSpec(
            num_scalar_prefetch=1,
            grid=(req_dev, heads // group),
            in_specs=[spec] * 3,
            out_specs=spec,
        ),
        out_shape=flat,
        cost_estimate=pl.CostEstimate(
            flops=8 * req_dev * heads * seq_len * seq_len * HD,
            bytes_accessed=8 * req_dev * seq_len * q_local,
            transcendentals=req_dev * heads * seq_len * seq_len,
        ),
    )(lengths, q, k, v)

    kv_cache = assemble(k, v, low, high, index, valid)
    return attended.reshape(req_dev, seq_len, q_local), kv_cache


def solution(mesh):
    in_specs = (
        P("req", None, None),
        P("req", None, "tp"),
        P("tp"),
        P("tp"),
        P("req"),
        P("req", None),
        P("req", None),
    )
    out_specs = (P("req", None, "tp"), P("req", None, None, "tp"))
    return jax.shard_map(body, mesh=mesh, in_specs=in_specs, out_specs=out_specs, check_vma=False)
```

time: 249 us -> 148 us (0.59); the launches traced: 245 us -> 147 us
  Pallas kernels: 0 us -> 118 us
  waiting for transfers between devices: 106 us -> 14.5 us
  local copies, waits for them, and re-layouts: 51 us -> 7.87 us
  matrix products: 33 us -> 0 us
  other arithmetic: 35.2 us -> 3.69 us
  between operations: 14.2 us -> 0.74 us
  blocking collectives: 3.82 us -> 0 us
    pallas_call x0 -> x5, Pallas kernels: none -> 118 us  [the longest x1 84.2 us: body(): pl.pallas_call(functools.partial(project_kernel, count, q_local * lax.axi...]
    all_gather x1 -> x0, waiting for transfers between devices: 106 us -> none  [body(): gathered = lax.all_gather(master_local, 'req', axis=0, tiled=True)]
    dot_general x6 -> x0, matrix products: 33 us -> none  [the longest x1 17.1 us: body(): jnp.dot(token_rows, gathered, preferred_element_type=jnp.float32)]
    unnamed x24 -> x8, local copies, waits for them, and re-layouts: 18.8 us -> 1.64 us
    ppermute x2, waiting for transfers between devices: 0.01 us -> 14.5 us  [the longest x1 10.6 us: body(): lax.ppermute(pack(k, v, index[2 * CAP:], valid[2 * CAP:]), 'req', forward)]
    sub x3 -> x0, other arithmetic: 14.2 us -> none  [the longest x2 12.6 us: attend(): exp_terms = jnp.where(allowed[None], jnp.exp(scores - row_max), 0.0)]
    dynamic_slice x6 -> x0, local copies, waits for them, and re-layouts: 6.79 us -> none  [body(): lax.map(attend, (q_rot, k_rot, v_round, lengths))]
    slice x4, local copies, waits for them, and re-layouts: 9.85 us -> 3.65 us  [the longest x1 1.3 us: body(): qkv_master[:, 1:]]
  transfers between devices with their start and end apart: 3 -> 2, of which waited for: 1 -> 2; matrix products, arithmetic and copies ran while one was open for 18% -> 2% of each run, Pallas kernels for 0% -> 14%
where the time goes in v1:
time: 148 us; the launch traced here: 147 us
  Pallas kernels  118 us (80%)
  waiting for transfers between devices  14.5 us (10%)
  local copies, waits for them, and re-layouts  7.87 us (5%)
  other arithmetic  3.69 us (2%)
  starting transfers between devices  2.37 us (2%)
    pallas_call x1, Pallas kernels, body(): pl.pallas_call(functools.partial(project_kernel, count, q_local * lax.axi...  84.2 us
    pallas_call x1, Pallas kernels, body(): pl.pallas_call(attention_kernel, grid_spec=pltpu.PrefetchScalarGridSpec(n...  17.2 us
    ppermute x1, waiting for transfers between devices, body(): lax.ppermute(pack(k, v, index[2 * CAP:], valid[2 * CAP:]), 'req', forward)  10.6 us
    pallas_call x1, Pallas kernels, assemble(): pl.pallas_call(assemble_kernel, grid_spec=pltpu.PrefetchScalarGridSpec(nu...  8.36 us
    pallas_call x2, Pallas kernels, pack(): pl.pallas_call(pack_kernel, grid_spec=pltpu.PrefetchScalarGridSpec(num_sc...  8.17 us
    ppermute x1, waiting for transfers between devices, body(): high = lax.ppermute(pack(k, v, index[:CAP], valid[:CAP]), 'req', backward)  3.94 us
  transfers between devices with their start and end apart: 2, of which 2 were waited for; matrix products, arithmetic and copies ran while one was open for 2% of the time, Pallas kernels for 14%

profile of v1, /device:TPU:1, one launch (start us, length us, event | category | flops | bytes accessed | tf_op | source)
XLA Modules:
  0.0 147.1 jit_solution(4597609564898438447)
XLA Ops:
  0.7 0.8 compare_select_fusion.2
  1.4 0.1 eq.17
  1.5 0.1 select_reduce_fusion
  1.6 0.1 fusion.1
  1.7 1.1 slice.39
  2.8 1.3 slice.38
  4.1 0.0 copy-start.2
  4.1 0.2 copy.13
  4.3 0.3 copy.14
  4.6 0.1 pad_maximum_fusion
  4.6 1.2 copy.12
  5.8 0.0 copy-done.2
  5.8 0.6 fusion.5
  6.4 1.0 fusion
  7.4 1.0 pad_maximum_fusion.1
  8.4 84.2 %shard_map.86 = (bf16[1024,1024]{1,0:T(8,128)(2,1)}, bf16[1024,1024]{1,0:T(8,128)(2,1)}, bf16[1024,1024]{1,0:T(8,128)(2,1)}) custom-call(bf16[1024,2048]{1,0:T(8,128)(2,1)} %bitcast.8, bf16[6,128,512]{2,1,0:T(8,128)(2,1)} %bitcast.10, f32[512,128]{1,0:T(8,128)} %get-tuple-element.18.cos_t, f32[512,128]{1,0:T(8,128)} %get-tuple-element.19.sin_t, ...), custom_call_target="tpu_custom_call" | custom-call | tf_op jit(solution)/shard_map/pallas_call | solution.py:319
  92.6 4.1 %shard_map.88 = bf16[3,2,128,1024]{3,2,1,0:T(8,128)(2,1)} custom-call(s32[3]{0:T(128)} %get-tuple-element.21.index, s32[3]{0:T(128)} %get-tuple-element.12.valid, bf16[1024,1024]{1,0:T(8,128)(2,1)} %get-tuple-element.6.k, bf16[1024,1024]{1,0:T(8,128)(2,1)} %get-tuple-element.7.v), custom_call_target="tpu_custom_call" | custom-call | tf_op jit(solution)/shard_map/pallas_call | solution.py:248
  96.7 2.4 %collective-permute-start = (bf16[3,2,128,1024]{3,2,1,0:T(8,128)(2,1)}, bf16[3,2,128,1024]{3,2,1,0:T(8,128)(2,1)S(1)}, u32[]{:S(2)}, u32[]{:S(2)}) collective-permute-start(bf16[3,2,128,1024]{3,2,1,0:T(8,128)(2,1)} %shard_map.88), channel_id=1, source_target_pairs={{0,2},{2,4},{4,6},{6,8},{8,10},{10,12},{12,14},{14,16},{16,18},{18... | collective-permute-start | bytes 4718600 | tf_op jit(solution)/shard_map/ppermute | solution.py:352
  99.1 4.1 %shard_map.89 = bf16[3,2,128,1024]{3,2,1,0:T(8,128)(2,1)} custom-call(s32[3]{0:T(128)} %get-tuple-element.22.index, s32[3]{0:T(128)} %get-tuple-element.11.valid, bf16[1024,1024]{1,0:T(8,128)(2,1)} %get-tuple-element.6.k, bf16[1024,1024]{1,0:T(8,128)(2,1)} %get-tuple-element.7.v), custom_call_target="tpu_custom_call" | custom-call | tf_op jit(solution)/shard_map/pallas_call | solution.py:248
  103.2 0.0 collective-permute-start.1
  103.2 0.7 fusion.7
  103.8 0.6 broadcast_in_dim.22
  104.5 0.7 broadcast_in_dim.23
  105.2 0.7 pad_add_fusion.index
  105.9 17.2 %shard_map.87 = bf16[1024,1024]{1,0:T(8,128)(2,1)} custom-call(s32[2]{0:T(128)} %lengths.1, bf16[1024,1024]{1,0:T(8,128)(2,1)} %get-tuple-element.5.q, bf16[1024,1024]{1,0:T(8,128)(2,1)} %get-tuple-element.6.k, bf16[1024,1024]{1,0:T(8,128)(2,1)} %get-tuple-element.7.v), custom_call_target="tpu_custom_call" | custom-call | flops 4294967296 | bytes 8388608 | tf_op jit(solution)/shard_map/pallas_call | solution.py:358
  123.0 10.6 %collective-permute-done.low = bf16[3,2,128,1024]{3,2,1,0:T(8,128)(2,1)S(1)} collective-permute-done((bf16[3,2,128,1024]{3,2,1,0:T(8,128)(2,1)}, bf16[3,2,128,1024]{3,2,1,0:T(8,128)(2,1)S(1)}, u32[]{:S(2)}, u32[]{:S(2)}) %collective-permute-start) | collective-permute-done | bytes 1572896 | tf_op jit(solution)/shard_map/ppermute | solution.py:352
  133.6 0.0 copy-start
  133.6 3.9 %collective-permute-done.1.high = bf16[3,2,128,1024]{3,2,1,0:T(8,128)(2,1)S(1)} collective-permute-done((bf16[3,2,128,1024]{3,2,1,0:T(8,128)(2,1)}, bf16[3,2,128,1024]{3,2,1,0:T(8,128)(2,1)S(1)}, u32[]{:S(2)}, u32[]{:S(2)}) %collective-permute-start.1) | collective-permute-done | bytes 1572896 | tf_op jit(solution)/shard_map/ppermute | solution.py:353
  137.6 0.0 copy-done
  137.6 0.0 copy-start.1
  137.6 1.2 copy-done.1
  138.8 8.4 %shard_map.90 = bf16[9,2,128,1024]{3,2,1,0:T(8,128)(2,1)} custom-call(s32[9]{0:T(128)} %pad_add_fusion.index, s32[9]{0:T(128)} %copy-done.2, bf16[1024,1024]{1,0:T(8,128)(2,1)} %get-tuple-element.6.k, bf16[1024,1024]{1,0:T(8,128)(2,1)} %get-tuple-element.7.v, bf16[3,2,128,1024]{3,2,1,0:T(8,128)(2,1)} %copy-done, bf16[3,2,128,1024]{3,2,1,0:T(8,128)(2,1)} %copy-done.1), custom_call_target="tpu_custom_call" | custom-call | tf_op jit(solution)/shard_map/pallas_call | solution.py:284
  (4 shorter events, 0.0 us)
Async XLA Ops:
  4.1 1.7 %copy-start.2 = (s32[9]{0:T(128)}, s32[9]{0:T(128)S(1)}, u32[]{:S(2)}) copy-start(s32[9]{0:T(128)S(1)} %convert_element_type.38.valid) | copy-start | bytes 112
  96.7 36.9 %collective-permute-start = (bf16[3,2,128,1024]{3,2,1,0:T(8,128)(2,1)}, bf16[3,2,128,1024]{3,2,1,0:T(8,128)(2,1)S(1)}, u32[]{:S(2)}, u32[]{:S(2)}) collective-permute-start(bf16[3,2,128,1024]{3,2,1,0:T(8,128)(2,1)} %shard_map.88), channel_id=1, source_target_pairs={{0,2},{2,4},{4,6},{6,8},{8,10},{10,12},{12,14},{14,16},{16,18},{18... | collective-permute-start | bytes 4718600 | tf_op jit(solution)/shard_map/ppermute | solution.py:352
  103.2 34.4 %collective-permute-start.1 = (bf16[3,2,128,1024]{3,2,1,0:T(8,128)(2,1)}, bf16[3,2,128,1024]{3,2,1,0:T(8,128)(2,1)S(1)}, u32[]{:S(2)}, u32[]{:S(2)}) collective-permute-start(bf16[3,2,128,1024]{3,2,1,0:T(8,128)(2,1)} %shard_map.89), channel_id=1, source_target_pairs={{2,0},{4,2},{6,4},{8,6},{10,8},{12,10},{14,12},{16,14},{18,16},{20... | collective-permute-start | bytes 4718600 | tf_op jit(solution)/shard_map/ppermute | solution.py:353
  133.6 3.9 %copy-start = (bf16[3,2,128,1024]{3,2,1,0:T(8,128)(2,1)}, bf16[3,2,128,1024]{3,2,1,0:T(8,128)(2,1)S(1)}, u32[]{:S(2)}) copy-start(bf16[3,2,128,1024]{3,2,1,0:T(8,128)(2,1)S(1)} %collective-permute-done.low) | copy-start | bytes 4718596
  137.6 1.2 copy-start.1

commit v2 on v1

v2 whole, which is shorter than its diff:
```python
import functools

import jax
import jax.numpy as jnp
import numpy as np
from jax import lax
from jax.experimental import pallas as pl
from jax.experimental.pallas import tpu as pltpu
from jax.sharding import PartitionSpec as P

HD = 128
PAGE = 128
CAP = 3
SLOTS = 9
STREAMS = 6
LAG = 2
MESH = pl.DeviceIdType.MESH
VMEM_LIMIT = 56 * 1024 * 1024

norm_epsilon = 1e-06
rope_theta = 500000.0


def prefill_kernel(
    n, full_width, seq_len,
    lengths, chosen, tok, master, cos_t, sin_t, q_gain, k_gain,
    attended, cache,
    weight, acc, q_rows, k_rows, v_rows, pages, ss_local, ss_remote,
    ring_send, ring_recv, sib_send, sib_recv, x_send, x_recv, page_send, page_recv, own_sem,
):
    rows = master.shape[1]
    half = weight.shape[2]
    token_rows, width = tok.shape
    chips = n // 2
    column = chips // 2
    me, tp = lax.axis_index("req"), lax.axis_index("tp")
    chip, core = me // 2, me % 2
    side, level = chip % 2, chip // 2
    place = level * (1 - side) + (chips - 1 - level) * side

    def chip_at(position):
        p = (position + 2 * chips) % chips
        u = p // column
        return 2 * (p * (1 - u) + (chips - 1 - p) * u) + u

    following = (chip_at(place + 1) * 2 + core, tp)
    preceding = (chip_at(place - 1) * 2 + core, tp)
    sibling = (chip * 2 + 1 - core, tp)
    other = (me, 1 - tp)
    onward = (following, preceding)
    before = ((me + n - 1) % n, tp)
    after = ((me + 1) % n, tp)

    def owner(direction, step):
        return chip_at(place - step + 2 * direction * step)

    def chunk(u, chip_index, core_index):
        start = pl.multiple_of((chip_index * 2 + core_index) * rows, 16)
        return weight.at[u, pl.ds(start, rows), :]

    def ring(u, step):
        piece = chunk(u, owner(u % 2, step - 1), core)
        return pltpu.make_async_remote_copy(
            piece, piece, ring_send.at[u, step], ring_recv.at[u, step],
            device_id=onward[u % 2], device_id_type=MESH,
        )

    def ring_in(u, step):
        piece = chunk(u, owner(u % 2, step), core)
        return pltpu.make_async_remote_copy(
            piece, piece, ring_send.at[u, step], ring_recv.at[u, step],
            device_id=onward[u % 2], device_id_type=MESH,
        )

    def sib(u, step, whose):
        piece = chunk(u, owner(u % 2, step), whose)
        return pltpu.make_async_remote_copy(
            piece, piece, sib_send.at[u, step], sib_recv.at[u, step],
            device_id=sibling, device_id_type=MESH,
        )

    fused = (2 * rows) % 256 == 0
    tile = 256

    def multiply(u, step):
        sib(u, step, 1 - core).wait_recv()
        if not fused:
            return
        start = pl.multiple_of(owner(u % 2, step) * 2 * rows, 256)

        def one(i, carry):
            at = pl.multiple_of(i * tile, tile)
            acc[u, pl.ds(at, tile), :] += jnp.dot(
                tok[pl.ds(at, tile), pl.ds(start, 2 * rows)],
                weight[u, pl.ds(start, 2 * rows), :],
                preferred_element_type=jnp.float32,
            )
            return carry

        lax.fori_loop(0, token_rows // tile, one, 0)

    own_start = pl.multiple_of(me * rows, 16)
    for u in range(STREAMS):
        at = (u % 2) * half
        weight[u, pl.ds(own_start, rows), :] = master[2 - u // 2, :, at : at + half].astype(jnp.bfloat16)

    barrier = pltpu.get_barrier_semaphore()
    for device in (following, preceding, sibling, other, before, after):
        pl.semaphore_signal(barrier, inc=1, device_id=device, device_id_type=MESH)
    pl.semaphore_wait(barrier, 6)

    for u in range(STREAMS):
        ring(u, 1).start()
    for u in range(STREAMS):
        sib(u, 0, core).start()

    def clear(i, carry):
        at = pl.multiple_of(i * 64, 64)
        for u in range(STREAMS):
            acc[u, pl.ds(at, 64), :] = jnp.zeros((64, half), jnp.float32)
        return carry

    lax.fori_loop(0, token_rows // 64, clear, 0)
    for u in range(STREAMS - LAG):
        multiply(u, 0)

    def middle(step, carry):
        for u in range(STREAMS):
            ring_in(u, step).wait_recv()
            ring(u, step + 1).start()
            sib(u, step, core).start()
            if u < LAG:
                multiply(u - LAG + STREAMS, step - 1)
            else:
                multiply(u - LAG, step)
        return carry

    lax.fori_loop(1, chips - 1, middle, 0)

    def whole(u):
        def one(i, carry):
            at = pl.multiple_of(i * tile, tile)
            acc[u, pl.ds(at, tile), :] = jnp.dot(
                tok[pl.ds(at, tile), :], weight[u], preferred_element_type=jnp.float32
            )
            return carry

        if not fused:
            lax.fori_loop(0, token_rows // tile, one, 0)

    block = 128

    def send_page(kind, direction, slot):
        return pltpu.make_async_remote_copy(
            pages.at[kind, 2 * direction, slot],
            cache.at[2 * direction * CAP + slot, kind],
            page_send.at[kind, direction, slot],
            page_recv.at[kind, direction, slot],
            device_id=(before, after)[direction], device_id_type=MESH,
        )

    def keep_page(kind, slot):
        return pltpu.make_async_copy(
            pages.at[kind, 1, slot], cache.at[CAP + slot, kind], own_sem.at[kind, slot]
        )

    candidates = token_rows // PAGE

    def publish(kind, source):
        for which in (0, 2, 1):

            def fill(i, carry, which=which):
                at = pl.multiple_of(i * 16, 16)
                sums = [None] * CAP
                for p in range(candidates):
                    rows_p = pl.ds(pl.multiple_of(p * PAGE + at, 16), 16)
                    page = source[rows_p, :]
                    for slot in range(CAP):
                        share = chosen[(which * CAP + slot) * candidates + p]
                        term = page * jnp.full(page.shape, share, jnp.float32).astype(page.dtype)
                        sums[slot] = term if p == 0 else sums[slot] + term
                for slot in range(CAP):
                    pages[kind, which, slot, pl.ds(at, 16), :] = sums[slot]
                return carry

            lax.fori_loop(0, PAGE // 16, fill, 0)
            for slot in range(CAP):
                if which == 1:
                    keep_page(kind, slot).start()
                else:
                    send_page(kind, which // 2, slot).start()

    def write_values(i, carry):
        at = pl.multiple_of(i * block, block)
        for part in range(2):
            v_rows[pl.ds(at, block), part * half : (part + 1) * half] = acc[
                part, pl.ds(at, block), :
            ].astype(jnp.bfloat16)
        return carry

    def values_ready():
        whole(0)
        whole(1)
        lax.fori_loop(0, token_rows // block, write_values, 0)
        publish(1, v_rows)

    last = chips - 1
    for u in range(STREAMS):
        ring_in(u, last).wait_recv()
        sib(u, last, core).start()
        if u < LAG:
            multiply(u - LAG + STREAMS, last - 1)
        else:
            multiply(u - LAG, last)
        if u - LAG == 1:
            values_ready()
    for u in range(STREAMS - LAG, STREAMS):
        multiply(u, last)
    for u in range(2, STREAMS):
        whole(u)

    lanes = lax.broadcasted_iota(jnp.int32, (block, 128), 1)

    def squares(i, carry):
        at = pl.multiple_of(i * block, block)

        def total(first_stream):
            a = acc[first_stream, pl.ds(at, block), :]
            b = acc[first_stream + 1, pl.ds(at, block), :]
            return jnp.sum(a * a + b * b, axis=-1, keepdims=True)

        placed = jnp.where(lanes == 0, total(4), jnp.where(lanes == 1, total(2), 0.0))
        ss_local[:, pl.ds(at, block)] = placed.T[:8, :]
        return carry

    lax.fori_loop(0, token_rows // block, squares, 0)
    exchange = pltpu.make_async_remote_copy(
        ss_local, ss_remote, x_send, x_recv, device_id=other, device_id_type=MESH
    )
    exchange.start()
    exchange.wait()

    def turn(base, lane, gain, out):
        def one(i, carry):
            at = pl.multiple_of(i * block, block)
            spot = pl.multiple_of((i * block) % seq_len, block)
            sums = ss_local[:, pl.ds(at, block)] + ss_remote[:, pl.ds(at, block)]
            scale = lax.rsqrt(sums / full_width + norm_epsilon)
            scale = jnp.concatenate([scale, jnp.zeros((block - 8, 128), jnp.float32)], 0).T
            cosine = cos_t[pl.ds(spot, block), :]
            sine = sin_t[pl.ds(spot, block), :]
            factor = scale[:, lane : lane + 1]
            for part in range(2):
                for c in range(half // HD):
                    h = slice(part * half + c * HD, part * half + (c + 1) * HD)
                    x = acc[base + part, pl.ds(at, block), c * HD : (c + 1) * HD]
                    x = x * factor * gain[:, h]
                    y = x * cosine + pltpu.roll(x, HD // 2, 1) * sine
                    out[pl.ds(at, block), h] = y.astype(jnp.bfloat16)
            return carry

        lax.fori_loop(0, token_rows // block, one, 0)

    turn(2, 1, k_gain, k_rows)
    publish(0, k_rows)
    turn(4, 0, q_gain, q_rows)

    heads = 2 * half // HD
    step_rows = 128

    def attend(i, carry):
        r, h = i // heads, i % heads
        length = lengths[r]
        top_row = pl.multiple_of(r * seq_len, seq_len)
        hs = pl.ds(pl.multiple_of(h * HD, HD), HD)
        for b in range(seq_len // step_rows):
            count = (b + 1) * step_rows
            rows_b = pl.ds(pl.multiple_of(top_row + b * step_rows, step_rows), step_rows)
            keys = pl.ds(top_row, count)
            scores = lax.dot_general(
                q_rows[rows_b, hs], k_rows[keys, hs], (((1,), (1,)), ((), ())),
                preferred_element_type=jnp.float32,
            ) * HD ** (-0.5)
            query_pos = lax.broadcasted_iota(jnp.int32, (step_rows, count), 0) + b * step_rows
            key_pos = lax.broadcasted_iota(jnp.int32, (step_rows, count), 1)
            allowed = (key_pos <= query_pos) & (key_pos < length)
            scores = jnp.where(allowed, scores, -1e30)
            terms = jnp.exp(scores - jnp.max(scores, axis=-1, keepdims=True))
            mixed = jnp.dot(
                terms.astype(jnp.bfloat16), v_rows[keys, hs], preferred_element_type=jnp.float32
            ) / jnp.sum(terms, axis=-1, keepdims=True)
            row = lax.broadcasted_iota(jnp.int32, (step_rows, HD), 0) + b * step_rows
            attended[rows_b, hs] = jnp.where(row < length, mixed, 0.0).astype(jnp.bfloat16)
        return carry

    lax.fori_loop(0, token_rows // seq_len * heads, attend, 0)

    def drain(step, carry):
        for u in range(STREAMS):
            ring(u, step).wait_send()
        return carry

    lax.fori_loop(1, chips, drain, 0)

    def drain_sib(step, carry):
        for u in range(STREAMS):
            sib(u, step, core).wait_send()
        return carry

    lax.fori_loop(0, chips, drain_sib, 0)
    for kind in (1, 0):
        for slot in range(CAP):
            for direction in range(2):
                send_page(kind, direction, slot).wait()
            keep_page(kind, slot).wait()


def body(tokens, qkv_master, q_gain, k_gain, lengths, page_holder, page_slot):
    req_dev, seq_len, model_width = tokens.shape
    row_share, _, q_local = qkv_master.shape
    half = q_local // 2
    count = lax.axis_size("req")
    chips = count // 2
    rows = req_dev * seq_len
    token_rows = tokens.reshape(rows, model_width)

    frequency = np.float32(rope_theta) ** (-np.arange(HD // 2, dtype=np.float32) * np.float32(2.0 / HD))
    angles = np.arange(seq_len, dtype=np.float32)[:, None] * frequency[None, :]
    cosine, sine = np.cos(angles), np.sin(angles)
    cosine = jnp.asarray(np.concatenate([cosine, cosine], -1), jnp.float32)
    sine = jnp.asarray(np.concatenate([-sine, sine], -1), jnp.float32)

    page_count = seq_len // PAGE
    home = lax.axis_index("req")
    live = (jnp.arange(page_count) * PAGE)[None, :] < lengths[:, None]
    offset = (page_holder - home + 1 + count) % count - 1
    target = jnp.where(live, (offset + 1) * CAP + page_slot, -1).reshape(-1)
    match = target[None, :] == jnp.arange(SLOTS)[:, None]
    chosen = match.astype(jnp.float32).reshape(-1)

    vmem = pl.BlockSpec(memory_space=pltpu.VMEM)
    smem = pl.BlockSpec(memory_space=pltpu.SMEM)
    dma = pltpu.SemaphoreType.DMA
    attended, cache = pl.pallas_call(
        functools.partial(prefill_kernel, count, q_local * lax.axis_size("tp"), seq_len),
        out_shape=(
            jax.ShapeDtypeStruct((rows, q_local), jnp.bfloat16),
            jax.ShapeDtypeStruct((SLOTS, 2, PAGE, q_local), jnp.bfloat16),
        ),
        in_specs=[smem] * 2 + [vmem] * 6,
        out_specs=(vmem, pl.BlockSpec(memory_space=pl.ANY)),
        scratch_shapes=[
            pltpu.VMEM((STREAMS, model_width, half), jnp.bfloat16),
            pltpu.VMEM((STREAMS, rows, half), jnp.float32),
            pltpu.VMEM((rows, q_local), jnp.bfloat16),
            pltpu.VMEM((rows, q_local), jnp.bfloat16),
            pltpu.VMEM((rows, q_local), jnp.bfloat16),
            pltpu.VMEM((2, 3, CAP, PAGE, q_local), jnp.bfloat16),
            pltpu.VMEM((8, rows), jnp.float32),
            pltpu.VMEM((8, rows), jnp.float32),
            dma((STREAMS, chips)), dma((STREAMS, chips)),
            dma((STREAMS, chips)), dma((STREAMS, chips)),
            dma, dma,
            dma((2, 2, CAP)), dma((2, 2, CAP)), dma((2, CAP)),
        ],
        compiler_params=pltpu.CompilerParams(
            collective_id=0, has_side_effects=True, vmem_limit_bytes=VMEM_LIMIT
        ),
    )(lengths, chosen, token_rows, qkv_master.transpose(1, 0, 2), cosine, sine, q_gain[None, :], k_gain[None, :])
    return attended.reshape(req_dev, seq_len, q_local), cache


def solution(mesh):
    in_specs = (
        P("req", None, None),
        P("req", None, "tp"),
        P("tp"),
        P("tp"),
        P("req"),
        P("req", None),
        P("req", None),
    )
    out_specs = (P("req", None, "tp"), P("req", None, None, "tp"))
    return jax.shard_map(body, mesh=mesh, in_specs=in_specs, out_specs=out_specs, check_vma=False)
```

time: 148 us -> 118 us (0.80)
  waiting for transfers between devices: 14.5 us -> 0 us
  Pallas kernels: 118 us -> 107 us
  other arithmetic: 3.69 us -> 0.78 us
  starting transfers between devices: 2.37 us -> 0 us
    ppermute x2 -> x0, waiting for transfers between devices: 14.5 us -> none  [the longest x1 10.6 us: body(): lax.ppermute(pack(k, v, index[2 * CAP:], valid[2 * CAP:]), 'req', forward)]
    pallas_call x5 -> x1, Pallas kernels: 118 us -> 107 us  [body(): pl.pallas_call(functools.partial(prefill_kernel, count, q_local * lax.axi...]
    unnamed x8 -> x2, local copies, waits for them, and re-layouts: 1.64 us -> 8.3 us
    slice x4 -> x0, local copies, waits for them, and re-layouts: 3.65 us -> none  [the longest x1 1.3 us: body(): qkv_master[:, 1:]]
    ppermute x2 -> x0, starting transfers between devices: 2.37 us -> none  [the longest x1 2.37 us: body(): lax.ppermute(pack(k, v, index[2 * CAP:], valid[2 * CAP:]), 'req', forward)]
    concatenate x3 -> x0, other arithmetic: 1.74 us -> none  [the longest x1 1 us: body(): cosine = jnp.concatenate([cosine, cosine], -1)]
  transfers between devices with their start and end apart: 2 -> 0, of which waited for: 2 -> 0; matrix products, arithmetic and copies ran while one was open for 2% -> 0% of each run, Pallas kernels for 14% -> 0%
where the time goes in v2:
time: 118 us
  Pallas kernels  107 us (91%)
  local copies, waits for them, and re-layouts  8.98 us (8%)
    pallas_call x1, Pallas kernels, body(): pl.pallas_call(functools.partial(prefill_kernel, count, q_local * lax.axi...  107 us
    unnamed x2, local copies, waits for them, and re-layouts  8.3 us

profile of v2, /device:TPU:1, one launch (start us, length us, event | category | flops | bytes accessed | tf_op | source)
XLA Modules:
  0.0 117.8 jit_solution(187801191783282542)
XLA Ops:
  0.6 0.8 compare_select_fusion.2
  1.4 0.1 eq.19
  1.5 0.6 reshape.24.chosen
  2.1 107.3 %shard_map.104 = (bf16[1024,1024]{1,0:T(8,128)(2,1)}, bf16[9,2,128,1024]{3,2,1,0:T(8,128)(2,1)}) custom-call(s32[2]{0:T(128)} %lengths.1, f32[72]{0:T(128)} %reshape.24.chosen, bf16[1024,2048]{1,0:T(8,128)(2,1)} %bitcast.5, f32[3,128,1024]{2,1,0:T(8,128)} %bitcast.7, f32[512,128]{1,0:T(8,128)} %constant.37.clone.cos_t, f32[512,128]{1,0:T(8,128)} %constant.38.clone.sin_t, ...), custom_call_target="tpu_custom_call" | custom-call | tf_op jit(solution)/shard_map/pallas_call | solution.py:344
  109.5 3.1 %copy.13 = bf16[2,512,1024]{2,1,0:T(8,128)(2,1)} copy(bf16[2,512,1024]{2,1,0:T(8,128)(2,1)} %bitcast.6) | data formatting | bytes 4194304
  112.5 5.2 %copy.14 = bf16[9,2,128,1024]{3,2,1,0:T(8,128)(2,1)} copy(bf16[9,2,128,1024]{3,2,1,0:T(8,128)(2,1)} %get-tuple-element.9) | data formatting | bytes 9437184
  (2 shorter events, 0.0 us)

commit v3 on v2

--- a/solution.py
+++ b/solution.py
@@ -1,4 +1,5 @@
 import functools
+import math
 
 import jax
 import jax.numpy as jnp
@@ -268,6 +269,11 @@
     heads = 2 * half // HD
     step_rows = 128
 
+    exponent = HD ** (-0.5) * math.log2(math.e)
+    below = lax.broadcasted_iota(jnp.int32, (step_rows, step_rows), 1) <= lax.broadcasted_iota(
+        jnp.int32, (step_rows, step_rows), 0
+    )
+
     def attend(i, carry):
         r, h = i // heads, i % heads
         length = lengths[r]
@@ -280,12 +286,12 @@
             scores = lax.dot_general(
                 q_rows[rows_b, hs], k_rows[keys, hs], (((1,), (1,)), ((), ())),
                 preferred_element_type=jnp.float32,
-            ) * HD ** (-0.5)
-            query_pos = lax.broadcasted_iota(jnp.int32, (step_rows, count), 0) + b * step_rows
-            key_pos = lax.broadcasted_iota(jnp.int32, (step_rows, count), 1)
-            allowed = (key_pos <= query_pos) & (key_pos < length)
-            scores = jnp.where(allowed, scores, -1e30)
-            terms = jnp.exp(scores - jnp.max(scores, axis=-1, keepdims=True))
+            )
+            key_pos = lax.broadcasted_iota(jnp.int32, (1, count), 1)
+            scores = scores + jnp.where(key_pos < length, 0.0, -1e30)
+            edge = jnp.where(below, scores[:, b * step_rows :], -1e30)
+            scores = edge if b == 0 else jnp.concatenate([scores[:, : b * step_rows], edge], 1)
+            terms = jnp.exp2((scores - jnp.max(scores, axis=-1, keepdims=True)) * exponent)
             mixed = jnp.dot(
                 terms.astype(jnp.bfloat16), v_rows[keys, hs], preferred_element_type=jnp.float32
             ) / jnp.sum(terms, axis=-1, keepdims=True)
@@ -293,7 +299,7 @@
             attended[rows_b, hs] = jnp.where(row < length, mixed, 0.0).astype(jnp.bfloat16)
         return carry
 
-    lax.fori_loop(0, token_rows // seq_len * heads, attend, 0)
+    lax.fori_loop(0, token_rows // seq_len * heads, attend, 0, unroll=2)
 
     def drain(step, carry):
         for u in range(STREAMS):

time: 118 us -> 118 us (level)
  no operation moved by 1% of the time
where the time goes in v3:
time: 118 us
  Pallas kernels  107 us (91%)
  local copies, waits for them, and re-layouts  8.98 us (8%)
    pallas_call x1, Pallas kernels, body(): pl.pallas_call(functools.partial(prefill_kernel, count, q_local * lax.axi...  107 us
    unnamed x2, local copies, waits for them, and re-layouts  8.3 us

profile of v3, /device:TPU:1, one launch (start us, length us, event | category | flops | bytes accessed | tf_op | source)
XLA Modules:
  0.0 117.8 jit_solution(10256447223765086276)
XLA Ops:
  0.6 0.8 compare_select_fusion.2
  1.4 0.1 eq.19
  1.5 0.6 reshape.24.chosen
  2.1 107.3 %shard_map.104 = (bf16[1024,1024]{1,0:T(8,128)(2,1)}, bf16[9,2,128,1024]{3,2,1,0:T(8,128)(2,1)}) custom-call(s32[2]{0:T(128)} %lengths.1, f32[72]{0:T(128)} %reshape.24.chosen, bf16[1024,2048]{1,0:T(8,128)(2,1)} %bitcast.5, f32[3,128,1024]{2,1,0:T(8,128)} %bitcast.7, f32[512,128]{1,0:T(8,128)} %constant.37.clone.cos_t, f32[512,128]{1,0:T(8,128)} %constant.38.clone.sin_t, ...), custom_call_target="tpu_custom_call" | custom-call | tf_op jit(solution)/shard_map/pallas_call | solution.py:350
  109.5 3.1 %copy.13 = bf16[2,512,1024]{2,1,0:T(8,128)(2,1)} copy(bf16[2,512,1024]{2,1,0:T(8,128)(2,1)} %bitcast.6) | data formatting | bytes 4194304
  112.5 5.2 %copy.14 = bf16[9,2,128,1024]{3,2,1,0:T(8,128)(2,1)} copy(bf16[9,2,128,1024]{3,2,1,0:T(8,128)(2,1)} %get-tuple-element.9) | data formatting | bytes 9437184
  (2 shorter events, 0.0 us)
